TPU v7x, 256 devices: a whole 4x4x8 slice. The times are simulated.
256 devices in a mesh: dp: 8 (over y, core), mp: 32 (over x, z).
Axes of the slice: x: 4, y: 4, z: 8, core: 2. Of those that a mesh axis runs over, the one named last changes fastest.
Arguments:
- tokens: bfloat16 [4096, 8192], P('dp', 'mp'), may hold values from -6 to 6
- base_weight: bfloat16 [8192, 8192], P(None, 'mp'), may hold values from -0.0625 to 0.0625
- adapter_pairs: bfloat16 [64, 8192, 128], P('mp'), as said below
- owner_map: int32 [64], replicated, may hold values from 0 to 63, each once
- seg_adapter: int32 [8, 4], replicated, may hold values from 0 to 63
- seg_lengths: int32 [8, 4], P('dp'), may hold values from 1 to 256, 512 in all within a row
- cotangent: bfloat16 [4096, 8192], P('dp', 'mp'), may hold values from -6 to 6
Outputs:
- output: bfloat16 [4096, 8192], P('dp', 'mp')
- input_grad: bfloat16 [4096, 8192], P('dp', 'mp')
- adapter_grad: float32 [64, 8192, 128], P('dp', 'mp')
Inputs may be any that keep to these rules, and one draw needn't show every extreme that they name: `owner_map`: slot p lives on mp index p // 2; every slot belongs to exactly one adapter. `adapter_pairs`: the first 64 columns of the last dimension hold the down projections, the last 64 the transposed up projections.
All inputs are finite; a program needn't handle non-finite values.
Results may differ from a plain program's by a relative error of at most 0.009.
Values may be sent and summed in bfloat16 or wider, within the bound.
A program may use at most 128 MiB of HBM per device.

v0:
```python
import jax
import jax.numpy as jnp
from jax import lax
from jax.sharding import PartitionSpec as P


def local(tokens, base_weight, adapter_pairs, owner_map, seg_adapter, seg_lengths, cotangent):
    tok_rows = tokens.shape[0]
    rank = adapter_pairs.shape[2] // 2
    segments = seg_lengths.shape[1]
    stored = adapter_pairs.shape[0]
    total_slots = stored * lax.axis_size("mp")
    adapter_count = owner_map.shape[0]
    batch_index = lax.axis_index("dp")
    ends = jnp.cumsum(seg_lengths[0])
    position = jnp.arange(tok_rows, dtype=jnp.int32)
    seg_row = jnp.sum((position[:, None] >= ends[None, :]).astype(jnp.int32), axis=1)
    mask_bf = (seg_row[:, None] == jnp.arange(segments, dtype=jnp.int32)[None, :]).astype(
        jnp.bfloat16
    )
    table_hit = jnp.arange(adapter_count, dtype=jnp.int32)[None, None, :] == seg_adapter[:, :, None]
    all_slots = jnp.sum(jnp.where(table_hit, owner_map[None, None, :], 0), axis=2)
    my_slots = lax.dynamic_slice_in_dim(all_slots, batch_index, 1, 0)[0]
    slices = lax.all_to_all(adapter_pairs, "mp", split_axis=1, concat_axis=0, tiled=True)
    seg_pairs = jnp.take(slices, my_slots, axis=0)
    down = seg_pairs[:, :, :rank]
    upper = seg_pairs[:, :, rank:]
    low_part = jnp.einsum("tf,sfr->tsr", tokens, down, preferred_element_type=jnp.float32)
    low_part = jnp.sum(low_part * mask_bf.astype(jnp.float32)[:, :, None], axis=1)
    back_part = jnp.einsum("tf,sfr->tsr", cotangent, upper, preferred_element_type=jnp.float32)
    back_part = jnp.sum(back_part * mask_bf.astype(jnp.float32)[:, :, None], axis=1)
    low_sum = lax.psum(low_part, "mp")
    low = low_sum.astype(jnp.bfloat16)
    low_masked = low[:, None, :] * mask_bf[:, :, None]
    weight_rows = base_weight
    base = jnp.dot(
        lax.all_gather(tokens, "mp", axis=1, tiled=True),
        weight_rows,
        preferred_element_type=jnp.float32,
    )
    output = (
        base + jnp.einsum("tsr,scr->tc", low_masked, upper, preferred_element_type=jnp.float32)
    ).astype(jnp.bfloat16)
    back_sum = lax.psum(back_part, "mp")
    back = back_sum.astype(jnp.bfloat16)
    back_masked = back[:, None, :] * mask_bf[:, :, None]
    weight_rows = base_weight
    summed = lax.psum_scatter(
        lax.dot_general(
            weight_rows, cotangent, (((1,), (1,)), ((), ())), preferred_element_type=jnp.float32
        ),
        "mp",
        scatter_dimension=0,
        tiled=True,
    )
    input_grad = (
        summed.T + jnp.einsum("tsr,sfr->tf", back_masked, down, preferred_element_type=jnp.float32)
    ).astype(jnp.bfloat16)
    grad_down = jnp.einsum("tf,tsr->sfr", tokens, back_masked, preferred_element_type=jnp.float32)
    grad_up = jnp.einsum("tf,tsr->sfr", cotangent, low_masked, preferred_element_type=jnp.float32)
    compact = jnp.concatenate([grad_down, grad_up], axis=-1)
    onehot = (jnp.arange(total_slots, dtype=jnp.int32)[:, None] == my_slots[None, :]).astype(
        jnp.float32
    )
    dense = jnp.einsum("ps,sfk->pfk", onehot, compact, precision=lax.Precision.HIGHEST)
    adapter_grad = lax.psum_scatter(dense, "dp", scatter_dimension=0, tiled=True)
    return (output, input_grad, adapter_grad)


def solution(mesh):
    in_specs = (
        P("dp", "mp"),
        P(None, "mp"),
        P("mp", None, None),
        P(),
        P(),
        P("dp", None),
        P("dp", "mp"),
    )
    out_specs = (P("dp", "mp"), P("dp", "mp"), P("dp", "mp", None))
    return jax.shard_map(local, mesh=mesh, in_specs=in_specs, out_specs=out_specs, check_vma=False)
```

profile of v0, /device:TPU:1, one launch (start us, length us, event | category | flops | bytes accessed | tf_op | source)
XLA Modules:
  0.0 609.0 jit_solution(3425868239730497435)
XLA Ops:
  8.0 0.0 all-gather.2.cloned.1.call-start
  8.1 0.7 all-gather.2.cloned.1.call-update
  8.7 10.1 %copy.43 = bf16[2,8192,128]{2,0,1:T(2,128)(2,1)} copy(bf16[2,8192,128]{2,1,0:T(8,128)(2,1)} %param.9) | data formatting | bytes 8388608 | tf_op args[2]
  18.9 12.1 %all-to-all-start = ((bf16[2,8192,128]{2,0,1:T(2,128)(2,1)}), bf16[2,8192,128]{2,0,1:T(2,128)(2,1)}, u32[]{:S(2)}, u32[]{:S(2)}) async-start(bf16[2,8192,128]{2,0,1:T(2,128)(2,1)} %copy.43), calls=%async_computation | async-start | bytes 8388608 | tf_op jit(solution)/shard_map/all_to_all | solution.py:24
  31.0 0.0 reduce-scatter.5.cloned.1.call-start
  31.1 0.2 reduce-window.8
  31.3 0.2 select_reduce_fusion
  31.5 0.2 dynamic-slice_reduce_fusion
  31.7 0.1 convert_reduce_fusion
  31.8 105.8 %all-to-all-done = bf16[2,8192,128]{2,0,1:T(2,128)(2,1)} async-done(((bf16[2,8192,128]{2,0,1:T(2,128)(2,1)}), bf16[2,8192,128]{2,0,1:T(2,128)(2,1)}, u32[]{:S(2)}, u32[]{:S(2)}) %all-to-all-start) | async-done | bytes 4194336 | tf_op jit(solution)/shard_map/all_to_all | solution.py:24
  137.6 2.7 copy.44
  140.4 2.2 copy.45
  142.6 2.8 gather_fusion
  145.4 0.1 copy.46
  145.5 0.1 broadcast_select_fusion
  145.6 0.3 fusion.7
  145.9 0.3 fusion.6
  146.2 124.6 %all-reduce.2 = (bf16[512,64]{0,1:T(8,128)(2,1)S(1)}, bf16[512,64]{0,1:T(8,128)(2,1)S(1)}) all-reduce(f32[512,64]{0,1:T(8,128)S(1)} %fusion.7, f32[512,64]{0,1:T(8,128)S(1)} %fusion.6), channel_id=1, replica_groups=mesh['dp'=8,'mp'=32] {'mp'}, use_global_device_ids=true, to_apply=%region_4.5 | all-reduce | flops 65536 | bytes 393216 | tf_op jit(solution)/shard_map/psum | solution.py:32
  270.8 0.2 convolution_bitcast_fusion.4
  271.0 0.2 convolution_bitcast_fusion.5
  271.3 0.2 copy.48
  271.5 5.8 fusion.30
  277.4 0.0 reduce-scatter.3.cloned.1.call-start
  277.4 10.3 %fusion.36 = f32[8192,512]{1,0:T(8,128)} fusion(bf16[8192,256]{1,0:T(8,128)(2,1)} %param.8, bf16[512,256]{1,0:T(8,128)(2,1)S(1)} %copy-done), kind=kOutput, calls=%fused_computation.55 | convolution fusion | flops 2147483648 | bytes 21233664 | tf_op jit(solution)/shard_map/dot_general | solution.py:49
  287.7 0.0 all-gather.2.cloned.1.call-done
  287.8 6.9 %fusion.35 = f32[512,256]{1,0:T(8,128)S(1)} fusion(bf16[512,8192]{1,0:T(8,128)(2,1)} %all-gather.2.cloned.1.call-done, bf16[8192,256]{1,0:T(8,128)(2,1)} %param.8), kind=kOutput, calls=%fused_computation.54 | convolution fusion | flops 2147483648 | bytes 13107200 | tf_op jit(solution)/shard_map/dot_general | solution.py:36
  294.7 1.0 fusion.5
  295.6 58.6 %reduce-scatter.5.cloned.1.call-done = f32[8,256,128]{2,0,1:T(8,128)} async-done(((f32[64,256,128]{2,0,1:T(8,128)}), f32[8,256,128]{2,0,1:T(8,128)}) %reduce-scatter.5.cloned.1.call-update) | async-done | bytes 1048592 | tf_op jit(solution)/shard_map/reduce_scatter | solution.py:66
  354.2 2.4 copy.50
  356.6 242.7 %reduce-scatter.3.cloned.1.call-done = f32[256,512]{1,0:T(8,128)} async-done(((f32[8192,512]{1,0:T(8,128)}), f32[256,512]{1,0:T(8,128)}) %reduce-scatter.3.cloned.1.call-update) | async-done | bytes 524304 | tf_op jit(solution)/shard_map/reduce_scatter | solution.py:48
  599.4 1.3 fusion.4
  600.7 0.8 copy.49
  (17 shorter events, 0.1 us)
Async XLA Ops:
  8.0 137.9 %copy-start = (bf16[512,256]{1,0:T(8,128)(2,1)S(1)}, bf16[512,256]{1,0:T(8,128)(2,1)}, u32[]{:S(2)}) copy-start(bf16[512,256]{1,0:T(8,128)(2,1)} %param.13) | copy-start | bytes 786436
  8.0 279.7 %all-gather.2.cloned.1.call-start = ((), (), s32[]{:S(2)}) async-start(), calls=%async_computation.3 | async-start | bytes 8650752 | tf_op jit(solution)/shard_map/all_gather | solution.py:37
  18.9 12.2 %copy-start.4 = (s32[1,4]{1,0:T(1,128)S(1)}, s32[1,4]{1,0:T(1,128)}, u32[]{:S(2)}) copy-start(s32[1,4]{1,0:T(1,128)} %param.12) | copy-start | bytes 52
  18.9 12.4 %copy-start.2 = (s32[8,4]{0,1:T(4,128)S(1)}, s32[8,4]{0,1:T(4,128)}, u32[]{:S(2)}) copy-start(s32[8,4]{0,1:T(4,128)} %param.11) | copy-start | bytes 388
  18.9 12.4 %copy-start.3 = (s32[64]{0:T(128)S(1)}, s32[64]{0:T(128)}, u32[]{:S(2)}) copy-start(s32[64]{0:T(128)} %param.10) | copy-start | bytes 772
  18.9 118.8 %all-to-all-start = ((bf16[2,8192,128]{2,0,1:T(2,128)(2,1)}), bf16[2,8192,128]{2,0,1:T(2,128)(2,1)}, u32[]{:S(2)}, u32[]{:S(2)}) async-start(bf16[2,8192,128]{2,0,1:T(2,128)(2,1)} %copy.43), calls=%async_computation | async-start | bytes 8388608 | tf_op jit(solution)/shard_map/all_to_all | solution.py:24
  31.0 323.2 %reduce-scatter.5.cloned.1.call-start = ((), (), s32[]{:S(2)}) async-start(), calls=%async_computation.5 | async-start | bytes 9437184 | tf_op jit(solution)/shard_map/reduce_scatter | solution.py:66
  140.3 5.3 copy-start.1
  277.4 322.0 %reduce-scatter.3.cloned.1.call-start = ((), (), s32[]{:S(2)}) async-start(), calls=%async_computation.4 | async-start | bytes 17301504 | tf_op jit(solution)/shard_map/reduce_scatter | solution.py:48
Sparse Core Ops, SparseCore 0:
  11.3 168.8 all-gather.1
Sparse Core Ops, SparseCore 1:
  277.5 76.7 reduce-scatter.4
  358.2 241.1 reduce-scatter.2
where the time goes:
time: 613 us; the launch traced here: 609 us
  waiting for transfers between devices  408 us (67%)
  blocking collectives  125 us (20%)
  matrix products  26.3 us (4%)
  local copies, waits for them, and re-layouts  21.6 us (4%)
  between operations  15.6 us (3%)
  starting transfers between devices  12.3 us (2%)
    reduce_scatter x1, waiting for transfers between devices, local(): lax.psum_scatter(lax.dot_general(weight_rows, cotangent, (((1,), (1,)), (...  243 us
    psum x1, blocking collectives, local(): low_sum = lax.psum(low_part, 'mp')  125 us
    all_to_all x1, waiting for transfers between devices, local(): lax.all_to_all(adapter_pairs, 'mp', split_axis=1, concat_axis=0, tiled=True)  106 us
    reduce_scatter x1, waiting for transfers between devices, local(): lax.psum_scatter(dense, 'dp', scatter_dimension=0, tiled=True)  58.6 us
    unnamed x13, local copies, waits for them, and re-layouts  13.4 us
  transfers between devices with their start and end apart: 4, of which 3 were waited for; matrix products, arithmetic and copies ran while one was open for 8% of the time, Pallas kernels for 0%

commit v1 on v0

v1 whole, which is shorter than its diff:
```python
import functools

import jax
import jax.numpy as jnp
from jax import lax
from jax.experimental import pallas as pl
from jax.experimental.pallas import tpu as pltpu
from jax.sharding import PartitionSpec as P

NZ = 8
CORES = 2
F32 = jnp.float32
BF16 = jnp.bfloat16
NT = (((1,), (1,)), ((), ()))
TN = (((0,), (0,)), ((), ()))


def dot(a, b, dims=(((1,), (0,)), ((), ()))):
    return lax.dot_general(a, b, dims, preferred_element_type=F32)


def hops(n, way, half):
    return n // 2 if way == half else n // 2 - 1


def kernel(
    nx, nz, ny,
    tok, cot, w, pairs, owner, seg, lens,
    out, ig, grad,
    T, C, Wb, S1, S2, sel, R, Lp, X1, Lz, Z1, Lf, Lm, acc, Pz, zs, zr, xs, xr, G,
    t_s, t_r, c_s, c_r, wx_s, wx_r, wy_s, wy_r, wc_s, wc_r,
    a1_s, a1_r, a2_s, a2_r, a3_s, a3_r,
    l1_s, l1_r, l2_s, l2_r, l3_s, l3_r, l4_s, l4_r,
    rz_s, rz_r, rx_s, rx_r, gy_s, gy_r, gc_s, gc_r, loc,
):
    nd = ny * CORES
    d = lax.axis_index("dp")
    j = lax.axis_index("mp")
    y, c = d // CORES, d % CORES
    x, z = j // nz, j % nz
    half_rows, feat = tok.shape[1], tok.shape[2]
    rows = 2 * half_rows
    lanes = 2 * (pairs.shape[-1] // 2)
    rank = lanes // 2
    segs = R.shape[0]
    sibling = (CORES * y + 1 - c, j)

    def at_x(r):
        return (d, lax.rem(r + nx, nx) * nz + z)

    def at_z(r):
        return (d, x * nz + lax.rem(r + nz, nz))

    def at_y(r):
        return (lax.rem(r + ny, ny) * CORES + c, j)

    def at_dp(r):
        return (lax.rem(r + nd, nd), j)

    pending = []

    def remote(src, dst, ssem, rsem, device):
        return pltpu.make_async_remote_copy(
            src_ref=src, dst_ref=dst, send_sem=ssem, recv_sem=rsem,
            device_id=device, device_id_type=pl.DeviceIdType.MESH,
        )

    def send(src, dst, ssem, rsem, device):
        copy = remote(src, dst, ssem, rsem, device)
        copy.start()
        pending.append(copy)

    def arrived(dst, ssem, rsem, device):
        remote(dst, dst, ssem, rsem, device).wait_recv()

    class Gather:
        def __init__(self, n, at, me, view, ssem, rsem, absolute=False):
            self.n, self.at, self.me, self.view = n, at, me, view
            self.ssem, self.rsem, self.absolute = ssem, rsem, absolute

        def send(self, way, half, step):
            sign = 1 - 2 * way
            src = self.view((-sign * (step - 1)) % self.n, half)
            dst = src if self.absolute else self.view((-sign * step) % self.n, half)
            k = (way, half, step - 1)
            send(src, dst, self.ssem.at[k], self.rsem.at[k], self.at(self.me + sign))

        def start(self):
            for way in range(2):
                for half in (way, 1 - way):
                    if hops(self.n, way, half) >= 1:
                        self.send(way, half, 1)

        def step(self, step, after=None):
            for half in range(2):
                for way in range(2):
                    if hops(self.n, way, half) >= step:
                        sign = 1 - 2 * way
                        off = (-sign * step) % self.n
                        k = (way, half, step - 1)
                        arrived(self.view(off, half), self.ssem.at[k], self.rsem.at[k],
                                self.at(self.me + sign))
                        if hops(self.n, way, half) >= step + 1:
                            self.send(way, half, step + 1)
                        if after is not None:
                            after(off, half)

    class Scatter:
        def __init__(self, n, at, me, part, sbuf, rbuf, ssem, rsem):
            self.n, self.at, self.me, self.part = n, at, me, part
            self.sbuf, self.rbuf, self.ssem, self.rsem = sbuf, rbuf, ssem, rsem

        def wait(self, way, half, i):
            k = (way, half, i)
            arrived(self.rbuf.at[k], self.ssem.at[k], self.rsem.at[k],
                    self.at(self.me + 1 - 2 * way))

        def step(self, i):
            for half in range(2):
                for way in range(2):
                    length = hops(self.n, way, half)
                    if i >= length:
                        continue
                    sign = 1 - 2 * way
                    k = (way, half, i)
                    value = self.part[(sign * (length - i)) % self.n, half]
                    if i > 0:
                        self.wait(way, half, i - 1)
                        value = value + self.rbuf[way, half, i - 1].astype(F32)
                    self.sbuf[k] = value.astype(BF16)
                    send(self.sbuf.at[k], self.rbuf.at[k], self.ssem.at[k], self.rsem.at[k],
                         self.at(self.me + sign))

        def finish(self, half):
            value = self.part[0, half]
            for way in range(2):
                length = hops(self.n, way, half)
                if length >= 1:
                    self.wait(way, half, length - 1)
                    value = value + self.rbuf[way, half, length - 1].astype(F32)
            return value

    own_w = pltpu.make_async_copy(w.at[x], Wb.at[0], loc.at[0])
    own_w.start()
    own_a = pltpu.make_async_copy(pairs.at[:, :, z, d], S1.at[pl.ds(2 * z, 2)], loc.at[1])
    own_a.start()
    T[0] = tok[...]
    C[0] = cot[...]

    barrier = pltpu.get_barrier_semaphore()
    partners = (
        [at_z(z + m) for m in range(1, nz)]
        + [at_x(x + m) for m in range(1, nx)]
        + [at_dp(d + m) for m in range(1, nd)]
    )
    for device in partners:
        pl.semaphore_signal(barrier, inc=1, device_id=device, device_id_type=pl.DeviceIdType.MESH)
    pl.semaphore_wait(barrier, len(partners))

    gather_t = Gather(nz, at_z, z, lambda off, h: T.at[off, h], t_s, t_r)
    gather_c = Gather(nx, at_x, x, lambda off, h: C.at[off, h], c_s, c_r)
    gather_w = Gather(
        ny, at_y, y,
        lambda off, h: Wb.at[pl.ds(1, nx - 1), lax.rem(y + off, ny) * CORES + c, h],
        wy_s, wy_r, absolute=True,
    )
    gather_g = Gather(
        ny, at_y, y,
        lambda off, h: G.at[CORES * off, :, pl.ds(h * (feat // 2), feat // 2)], gy_s, gy_r,
    )
    scatter_z = Scatter(nz, at_z, z, Pz, zs, zr, rz_s, rz_r)
    scatter_x = Scatter(nx, at_x, x, acc, xs, xr, rx_s, rx_r)

    def w_piece(off, core, h):
        return Wb.at[pl.ds(1, nx - 1), lax.rem(y + off, ny) * CORES + core, h]

    def w_share(off, h):
        piece = w_piece(off, c, h)
        send(piece, piece, wc_s.at[off, h], wc_r.at[off, h], sibling)

    def g_piece(off, core, h):
        return G.at[CORES * off + core, :, pl.ds(h * (feat // 2), feat // 2)]

    def g_share(off, h):
        send(g_piece(off, 0, h), g_piece(off, 1, h), gc_s.at[off, h], gc_r.at[off, h], sibling)

    for k in range(1, nx):
        send(w.at[lax.rem(x - k + nx, nx), d], Wb.at[k, d], wx_s.at[k], wx_r.at[k], at_x(x - k))
    for m in range(1, nz):
        send(pairs.at[:, :, lax.rem(z + m, nz), d], S1.at[pl.ds(2 * z, 2)],
             a1_s.at[m], a1_r.at[m], at_z(z + m))
    gather_t.start()
    gather_c.start()

    for k in range(1, nx):
        arrived(Wb.at[k, d], wx_s.at[k], wx_r.at[k], at_x(x - k))
    gather_w.start()
    for h in range(2):
        w_share(0, h)
    gather_t.step(1)
    gather_c.step(1)

    own_a.wait()
    for m in range(1, nz):
        src = lax.rem(z - m + nz, nz)
        arrived(S1.at[pl.ds(2 * src, 2)], a1_s.at[m], a1_r.at[m], at_z(z + m))
    for k in range(1, nx):
        send(S1.at[:, lax.rem(x + k, nx)], S2.at[pl.ds(2 * nz * x, 2 * nz)],
             a2_s.at[k], a2_r.at[k], at_x(x + k))
    S2[pl.ds(2 * nz * x, 2 * nz)] = S1[:, x]
    gather_w.step(1, w_share)
    gather_t.step(2)
    for s in range(2, nx // 2 + 1):
        gather_c.step(s)
    for k in range(1, nx):
        src = lax.rem(x - k + nx, nx)
        arrived(S2.at[pl.ds(2 * nz * src, 2 * nz)], a2_s.at[k], a2_r.at[k], at_x(x + k))

    for m in range(nd):
        other = lax.rem(d + m, nd)
        for s in range(segs):
            sel[m, s] = S2[owner[seg[other, s]]]
        if m > 0:
            send(sel.at[m], R.at[:, d], a3_s.at[m], a3_r.at[m], at_dp(d + m))
    R[:, d] = sel[0]
    for s in range(2, ny // 2 + 1):
        gather_w.step(s, w_share)
    for m in range(1, nd):
        src = lax.rem(d - m + nd, nd)
        arrived(R.at[:, src], a3_s.at[m], a3_r.at[m], at_dp(d + m))

    row = lax.broadcasted_iota(jnp.int32, (rows, lanes), 0)
    lane = lax.broadcasted_iota(jnp.int32, (rows, lanes), 1)
    starts = [jnp.int32(0)]
    for s in range(segs):
        starts.append(starts[-1] + lens[0, s])

    def mask(s):
        return (row >= starts[s]) & (row < starts[s + 1])

    tok2 = tok[...].reshape(rows, feat)
    cot2 = cot[...].reshape(rows, feat)
    part = jnp.zeros((rows, lanes), F32)
    for s in range(segs):
        pair = R[s].reshape(feat, lanes)
        both = jnp.where(lane < rank, dot(tok2, pair), dot(cot2, pair))
        part = part + jnp.where(mask(s), both, 0.0)
    Lp[...] = part.reshape(Lp.shape)
    for k in range(1, nx):
        send(Lp.at[lax.rem(x + k, nx)], X1.at[k], l1_s.at[k], l1_r.at[k], at_x(x + k))

    own_w.wait()
    for off in range(ny):
        for h in range(2):
            arrived(w_piece(off, 1 - c, h), wc_s.at[off, h], wc_r.at[off, h], sibling)

    def partial_ig(off):
        tile = lax.rem(z + off, nz)
        total = jnp.zeros((rows, feat), F32)
        for k in range(nx):
            total = total + dot(C[k].reshape(rows, feat), Wb[k, tile].reshape(feat, feat), NT)
        Pz[off] = total.reshape(2, half_rows, feat)

    def far_body(i, carry):
        partial_ig(i + nz // 2 - 1)
        return carry

    lax.fori_loop(0, 3, far_body, 0)
    scatter_z.step(0)

    for k in range(1, nx):
        arrived(X1.at[k], l1_s.at[k], l1_r.at[k], at_x(x + k))
    total = Lp[x]
    for k in range(1, nx):
        total = total + X1[k]
    Lz[...] = total.reshape(Lz.shape)
    for m in range(1, nz):
        send(Lz.at[lax.rem(z + m, nz)], Z1.at[m], l2_s.at[m], l2_r.at[m], at_z(z + m))
    gather_t.step(3)

    def near_body(i, carry):
        partial_ig(lax.rem(i + nz // 2 + 2, nz))
        return carry

    lax.fori_loop(0, nz - 3, near_body, 0)

    for m in range(1, nz):
        arrived(Z1.at[m], l2_s.at[m], l2_r.at[m], at_z(z + m))
    total = Lz[z]
    for m in range(1, nz):
        total = total + Z1[m]
    Lf[x, z] = pltpu.roll(total, rank, 1).astype(BF16)
    for m in range(1, nz):
        send(Lf.at[x, z], Lf.at[x, z], l3_s.at[m], l3_r.at[m], at_z(z + m))
    scatter_z.step(1)

    def partial_out(m, first):
        tile = lax.rem(z + m, nz)
        block = T[m].reshape(rows, feat)

        def body(k, carry):
            value = dot(block, Wb[k, tile].reshape(feat, feat)).reshape(2, half_rows, feat)
            acc[k] = value if first else acc[k] + value
            return carry

        lax.fori_loop(0, nx, body, 0)

    partial_out(0, True)

    def near_out(i, carry):
        partial_out(lax.rem(jnp.where(i < 2, i + nz - 2, i - 1), nz), False)
        return carry

    near = 4 if nz > 4 else 2
    if nz > 4:
        lax.fori_loop(0, 4, near_out, 0)

    for m in range(1, nz):
        src = lax.rem(z - m + nz, nz)
        arrived(Lf.at[x, src], l3_s.at[m], l3_r.at[m], at_z(z + m))
    for k in range(1, nx):
        send(Lf.at[x], Lf.at[x], l4_s.at[k], l4_r.at[k], at_x(x + k))

    for s in range(4, nz // 2 + 1):
        gather_t.step(s)

    def far_out(i, carry):
        if nz > 4:
            partial_out(i + 3, False)
        else:
            partial_out(i + 1, False)
        return carry

    lax.fori_loop(0, nz - 5 if nz > 4 else nz - 1, far_out, 0)
    scatter_x.step(0)
    if nz // 2 > 2:
        scatter_z.step(2)

    for k in range(1, nx):
        src = lax.rem(x - k + nx, nx)
        arrived(Lf.at[src], l4_s.at[k], l4_r.at[k], at_x(x + k))
    both = Lf[...].reshape(rows, lanes)
    for s in range(segs):
        Lm[:, s * lanes:(s + 1) * lanes] = jnp.where(mask(s), both, jnp.zeros_like(both))
    g_tok = dot(tok2, Lm[...], TN)
    g_cot = dot(cot2, Lm[...], TN)
    g_lane = lax.broadcasted_iota(jnp.int32, (feat, lanes), 1)
    for s in range(segs):
        part_s = slice(s * lanes, (s + 1) * lanes)
        G[0, s] = jnp.where(g_lane < rank, g_tok[:, part_s], g_cot[:, part_s]).astype(BF16)
    gather_g.start()
    for h in range(2):
        g_share(0, h)

    fix_out = jnp.zeros((rows, feat), F32)
    fix_ig = jnp.zeros((rows, feat), F32)
    for s in range(segs):
        pair = R[s].reshape(feat, lanes)
        mine = Lm[:, s * lanes:(s + 1) * lanes]
        zero = jnp.zeros_like(mine)
        fix_out = fix_out + dot(jnp.where(lane < rank, zero, mine), pair, NT)
        fix_ig = fix_ig + dot(jnp.where(lane < rank, mine, zero), pair, NT)
    acc[0] = acc[0] + fix_out.reshape(2, half_rows, feat)
    Pz[0] = Pz[0] + fix_ig.reshape(2, half_rows, feat)

    for i in range(1, nx // 2):
        scatter_x.step(i)
    for i in range(3, nz // 2):
        scatter_z.step(i)
    gather_g.step(1, g_share)

    slots = grad.shape[0]
    chunk = min(32, feat)

    def add_grads(i, first):
        off, core = i // CORES, i % CORES
        src = lax.rem(y + off, ny) * CORES + jnp.where(core == 0, c, 1 - c)
        hit = [[(owner[seg[src, s]] == slots * d + q).astype(F32) for s in range(segs)]
               for q in range(slots)]

        def body(r, carry):
            at = pl.ds(pl.multiple_of(r * chunk, chunk), chunk)
            given = [G[i, s, at].astype(F32) for s in range(segs)]
            for q in range(slots):
                value = given[0] * hit[q][0]
                for s in range(1, segs):
                    value = value + given[s] * hit[q][s]
                grad[q, at] = value if first else grad[q, at] + value
            return carry

        lax.fori_loop(0, feat // chunk, body, 0)

    add_grads(0, True)

    for h in range(2):
        out[h] = scatter_x.finish(h).astype(BF16)

    def g_wait(off):
        for h in range(2):
            arrived(g_piece(off, 1, h), gc_s.at[off, h], gc_r.at[off, h], sibling)

    for s in range(2, ny // 2 + 1):
        gather_g.step(s, g_share)
    for off in range(ny):
        g_wait(off)

    def grads_body(i, carry):
        add_grads(i, False)
        return carry

    lax.fori_loop(1, nd, grads_body, 0)

    for h in range(2):
        ig[h] = scatter_z.finish(h).astype(BF16)

    for copy in pending:
        copy.wait_send()


def local(tokens, base_weight, adapter_pairs, owner_map, seg_adapter, seg_lengths, cotangent):
    rows, feat = tokens.shape
    half = rows // 2
    nz = NZ
    nx = lax.axis_size("mp") // nz
    ny = lax.axis_size("dp") // CORES
    nd = ny * CORES
    stored, depth, lanes = adapter_pairs.shape
    segs = seg_lengths.shape[1]
    total_slots = stored * nx * nz
    slots = total_slots // nd
    piece = feat // nd
    lrows = rows // (nx * nz)
    vmem = lambda shape, dtype: pltpu.VMEM(shape, dtype)
    dma = lambda *shape: pltpu.SemaphoreType.DMA(shape)
    ring = lambda n: [dma(2, 2, n // 2)] * 2
    pair = lambda *shape: [dma(*shape)] * 2
    scratch = [
        vmem((nz, 2, half, feat), BF16),
        vmem((nx, 2, half, feat), BF16),
        vmem((nx, nz, 2, feat // 2, feat), BF16),
        vmem((stored * nz, nx, piece, lanes), BF16),
        vmem((total_slots, piece, lanes), BF16),
        vmem((nd, segs, piece, lanes), BF16),
        vmem((segs, nd, piece, lanes), BF16),
        vmem((nx, rows // nx, lanes), F32),
        vmem((nx, rows // nx, lanes), F32),
        vmem((nz, lrows, lanes), F32),
        vmem((nz, lrows, lanes), F32),
        vmem((nx, nz, lrows, lanes), BF16),
        vmem((rows, segs * lanes), BF16),
        vmem((nx, 2, half, feat), F32),
        vmem((nz, 2, half, feat), F32),
        vmem((2, 2, nz // 2, half, feat), BF16),
        vmem((2, 2, nz // 2, half, feat), BF16),
        vmem((2, 2, nx // 2, half, feat), BF16),
        vmem((2, 2, nx // 2, half, feat), BF16),
        vmem((nd, segs, feat, lanes), BF16),
        *ring(nz), *ring(nx), *pair(nx), *ring(ny), *pair(ny, 2),
        *pair(nz), *pair(nx), *pair(nd),
        *pair(nx), *pair(nz), *pair(nz), *pair(nx),
        *ring(nz), *ring(nx), *ring(ny), *pair(ny, 2), dma(2),
    ]
    in_vmem = pl.BlockSpec(memory_space=pltpu.VMEM)
    in_smem = pl.BlockSpec(memory_space=pltpu.SMEM)
    in_any = pl.BlockSpec(memory_space=pl.ANY)
    out, ig, grad = pl.pallas_call(
        functools.partial(kernel, nx, nz, ny),
        out_shape=[
            jax.ShapeDtypeStruct((2, half, feat), BF16),
            jax.ShapeDtypeStruct((2, half, feat), BF16),
            jax.ShapeDtypeStruct((slots, feat, lanes), F32),
        ],
        in_specs=[in_vmem, in_vmem, in_any, in_any, in_smem, in_smem, in_smem],
        out_specs=[in_vmem] * 3,
        scratch_shapes=scratch,
        compiler_params=pltpu.CompilerParams(
            collective_id=0, has_side_effects=True, vmem_limit_bytes=56 * 1024 * 1024
        ),
    )(
        tokens.reshape(2, half, feat),
        cotangent.reshape(2, half, feat),
        base_weight.reshape(nx, nz, 2, feat // 2, feat),
        adapter_pairs.reshape(stored, nx, nz, nd, piece, lanes),
        owner_map,
        seg_adapter,
        seg_lengths,
    )
    return out.reshape(rows, feat), ig.reshape(rows, feat), grad


def solution(mesh):
    in_specs = (
        P("dp", "mp"),
        P(None, "mp"),
        P("mp", None, None),
        P(),
        P(),
        P("dp", None),
        P("dp", "mp"),
    )
    out_specs = (P("dp", "mp"), P("dp", "mp"), P("dp", "mp", None))
    return jax.shard_map(local, mesh=mesh, in_specs=in_specs, out_specs=out_specs, check_vma=False)
```

time: 613 us -> 95.8 us (0.16)
  waiting for transfers between devices: 408 us -> 0 us
  blocking collectives: 125 us -> 0 us
  Pallas kernels: 0 us -> 88 us
  matrix products: 26.3 us -> 0 us
  between operations: 15.6 us -> 0.64 us
  local copies, waits for them, and re-layouts: 21.6 us -> 6.96 us
  starting transfers between devices: 12.3 us -> 0 us
    reduce_scatter x2 -> x0, waiting for transfers between devices: 301 us -> none  [the longest x1 243 us: local(): lax.psum_scatter(lax.dot_general(weight_rows, cotangent, (((1,), (1,)), (...]
    psum x1 -> x0, blocking collectives: 125 us -> none  [local(): low_sum = lax.psum(low_part, 'mp')]
    all_to_all x1 -> x0, waiting for transfers between devices: 106 us -> none  [local(): lax.all_to_all(adapter_pairs, 'mp', split_axis=1, concat_axis=0, tiled=True)]
    pallas_call x0 -> x1, Pallas kernels: none -> 88 us  [local(): pl.pallas_call(functools.partial(kernel, nx, nz, ny), out_shape=[jax.Shap...]
    dot_general x9 -> x0, matrix products: 26.3 us -> none  [the longest x1 10.3 us: local(): lax.dot_general(weight_rows, cotangent, (((1,), (1,)), ((), ())), preferr...]
    all_to_all x1 -> x0, starting transfers between devices: 12.1 us -> none  [local(): lax.all_to_all(adapter_pairs, 'mp', split_axis=1, concat_axis=0, tiled=True)]
    unnamed x13 -> x4, local copies, waits for them, and re-layouts: 13.4 us -> 6.96 us
  transfers between devices with their start and end apart: 4 -> 0, of which waited for: 3 -> 0; matrix products, arithmetic and copies ran while one was open for 8% -> 0% of each run, Pallas kernels for 0% -> 0%
where the time goes in v1:
time: 95.8 us; the launch traced here: 95.6 us
  Pallas kernels  88 us (92%)
  local copies, waits for them, and re-layouts  6.96 us (7%)
    pallas_call x1, Pallas kernels, local(): pl.pallas_call(functools.partial(kernel, nx, nz, ny), out_shape=[jax.Shap...  88 us
    unnamed x4, local copies, waits for them, and re-layouts  6.96 us

profile of v1, /device:TPU:1, one launch (start us, length us, event | category | flops | bytes accessed | tf_op | source)
XLA Modules:
  0.0 95.6 jit_solution(11831089337789472256)
XLA Ops:
  0.6 1.3 %copy.10.seg = s32[8,4]{1,0:T(8,128)} copy(s32[8,4]{0,1:T(4,128)} %param.11) | data formatting | bytes 256 | tf_op args[4]
  2.0 88.0 %shard_map.94 = (bf16[2,256,256]{2,1,0:T(8,128)(2,1)}, bf16[2,256,256]{2,1,0:T(8,128)(2,1)}, f32[8,256,128]{2,1,0:T(8,128)}) custom-call(bf16[2,256,256]{2,1,0:T(8,128)(2,1)} %bitcast.8, bf16[2,256,256]{2,1,0:T(8,128)(2,1)} %bitcast.9, bf16[4,8,2,128,256]{4,3,2,1,0:T(8,128)(2,1)} %bitcast.6, bf16[2,4,8,8,32,128]{5,4,3,2,1,0:T(8,128)(2,1)} %bitcast.7, ...), custom_call_target="tpu_custom_call" | custom-call | tf_op jit(solution)/shard_map/pallas_call | solution.py:466
  90.0 1.7 %copy.14 = bf16[512,256]{1,0:T(8,128)(2,1)} copy(bf16[512,256]{1,0:T(8,128)(2,1)} %bitcast.11) | data formatting | bytes 524288
  91.6 1.7 %copy.15 = bf16[512,256]{1,0:T(8,128)(2,1)} copy(bf16[512,256]{1,0:T(8,128)(2,1)} %bitcast.10) | data formatting | bytes 524288
  93.3 2.3 %copy.16 = f32[8,256,128]{2,1,0:T(8,128)} copy(f32[8,256,128]{2,1,0:T(8,128)} %get-tuple-element.14) | data formatting | bytes 2097152

commit v2 on v0

v2 whole, which is shorter than its diff:
```python
import functools

import jax
import jax.numpy as jnp
from jax import lax
from jax.experimental import pallas as pl
from jax.experimental.pallas import tpu as pltpu
from jax.sharding import PartitionSpec as P

NZ = 8
CORES = 2
QT = 1
QI = 1
F32 = jnp.float32
BF16 = jnp.bfloat16
SCHEDULE = "WLTWCLWCTWTLCTTWWLCiiTooITLIoIoiTLoIOIOGiOISiGIFGSSOI"
NT = (((1,), (1,)), ((), ()))
TN = (((0,), (0,)), ((), ()))


def dot(a, b, dims=(((1,), (0,)), ((), ()))):
    return lax.dot_general(a, b, dims, preferred_element_type=F32)


def hops(n, way, half):
    return n // 2 if way == half else n // 2 - 1


def kernel(
    nx, nz, ny,
    tok, cot, w, pairs, owner, seg, lens,
    out, ig, grad,
    T, C, Wb, S2, sel, R, Lp, X1, Lz, Z1, Lf, Lm, acc, Pz, zs, zr, xs, xr, G,
    t_s, t_r, c_s, c_r, wx_s, wx_r, wy_s, wy_r, wc_s, wc_r,
    a1_s, a1_r, a3_s, a3_r, lx_s, lx_r, lz_s, lz_r, l2_s, l2_r,
    rz_s, rz_r, rx_s, rx_r, gy_s, gy_r, gc_s, gc_r, loc,
):
    nd = ny * CORES
    d = lax.axis_index("dp")
    j = lax.axis_index("mp")
    y, c = d // CORES, d % CORES
    x, z = j // nz, j % nz
    half_rows, feat = tok.shape[1], tok.shape[2]
    rows = 2 * half_rows
    lanes = 2 * (pairs.shape[-1] // 2)
    rank = lanes // 2
    segs = R.shape[0]
    sibling = (CORES * y + 1 - c, j)

    def at_x(r):
        return (d, lax.rem(r + nx, nx) * nz + z)

    def at_z(r):
        return (d, x * nz + lax.rem(r + nz, nz))

    def at_y(r):
        return (lax.rem(r + ny, ny) * CORES + c, j)

    def at_dp(r):
        return (lax.rem(r + nd, nd), j)

    pending = []

    def remote(src, dst, ssem, rsem, device):
        return pltpu.make_async_remote_copy(
            src_ref=src, dst_ref=dst, send_sem=ssem, recv_sem=rsem,
            device_id=device, device_id_type=pl.DeviceIdType.MESH,
        )

    def send(src, dst, ssem, rsem, device):
        copy = remote(src, dst, ssem, rsem, device)
        copy.start()
        pending.append(copy)

    def arrived(dst, ssem, rsem, device):
        remote(dst, dst, ssem, rsem, device).wait_recv()

    class Fan:
        def __init__(self, count, at, src, dst, landed, ssem, rsem):
            self.count, self.at, self.src, self.dst, self.landed = count, at, src, dst, landed
            self.ssem, self.rsem = ssem, rsem

        def start(self):
            for m in range(1, self.count):
                send(self.src(m), self.dst(m), self.ssem.at[m], self.rsem.at[m], self.at(m))

        def wait(self):
            for m in range(1, self.count):
                arrived(self.landed(m), self.ssem.at[m], self.rsem.at[m], self.at(m))

    class Gather:
        def __init__(self, n, at, me, view, ssem, rsem, absolute=False):
            self.n, self.at, self.me, self.view = n, at, me, view
            self.ssem, self.rsem, self.absolute = ssem, rsem, absolute
            self.pieces = ssem.shape[2]

        def send(self, way, half, piece, step):
            sign = 1 - 2 * way
            src = self.view((-sign * (step - 1)) % self.n, half, piece)
            dst = src if self.absolute else self.view((-sign * step) % self.n, half, piece)
            k = (way, half, piece, step - 1)
            send(src, dst, self.ssem.at[k], self.rsem.at[k], self.at(self.me + sign))

        def start(self):
            for turn in range(2):
                for piece in range(self.pieces):
                    for way in range(2):
                        half = way if turn == 0 else 1 - way
                        if hops(self.n, way, half) >= 1:
                            self.send(way, half, piece, 1)

        def turns(self, step):
            return [turn for turn in range(2) if hops(self.n, 0, turn) >= step]

        def step(self, step, turn, after=None):
            for piece in range(self.pieces):
                for way in range(2):
                    half = way if turn == 0 else 1 - way
                    sign = 1 - 2 * way
                    off = (-sign * step) % self.n
                    k = (way, half, piece, step - 1)
                    arrived(self.view(off, half, piece), self.ssem.at[k], self.rsem.at[k],
                            self.at(self.me + sign))
                    if hops(self.n, way, half) >= step + 1:
                        self.send(way, half, piece, step + 1)
                    if after is not None:
                        after(off, half)

        def steps(self, after=None):
            self.start()
            yield
            for step in range(1, self.n // 2 + 1):
                for turn in self.turns(step):
                    self.step(step, turn, after)
                    yield

    class Scatter:
        def __init__(self, n, at, me, part, sbuf, rbuf, ssem, rsem):
            self.n, self.at, self.me, self.part = n, at, me, part
            self.sbuf, self.rbuf, self.ssem, self.rsem = sbuf, rbuf, ssem, rsem
            self.pieces = ssem.shape[2]
            self.size = part.shape[2] // self.pieces

        def rows(self, piece):
            return pl.ds(piece * self.size, self.size)

        def wait(self, way, half, piece, i):
            k = (way, half, piece, i)
            arrived(self.rbuf.at[way, half, i, self.rows(piece)], self.ssem.at[k],
                    self.rsem.at[k], self.at(self.me + 1 - 2 * way))

        def step(self, i, turn):
            for piece in range(self.pieces):
                for way in range(2):
                    half = way if turn == 0 else 1 - way
                    length = hops(self.n, way, half)
                    sign = 1 - 2 * way
                    k = (way, half, piece, i)
                    at = self.rows(piece)
                    value = self.part[(sign * (length - i)) % self.n, half, at]
                    if i > 0:
                        self.wait(way, half, piece, i - 1)
                        value = value + self.rbuf[way, half, i - 1, at].astype(F32)
                    self.sbuf[way, half, i, at] = value.astype(BF16)
                    send(self.sbuf.at[way, half, i, at], self.rbuf.at[way, half, i, at],
                         self.ssem.at[k], self.rsem.at[k], self.at(self.me + sign))

        def steps(self, result):
            for i in range(self.n // 2):
                for turn in range(2):
                    if i < hops(self.n, 0, turn):
                        self.step(i, turn)
                        yield
            for half in range(2):
                for piece in range(self.pieces):
                    result[half, self.rows(piece)] = self.finish(half, piece)
            yield

        def finish(self, half, piece):
            at = self.rows(piece)
            value = self.part[0, half, at]
            for way in range(2):
                length = hops(self.n, way, half)
                if length >= 1:
                    self.wait(way, half, piece, length - 1)
                    value = value + self.rbuf[way, half, length - 1, at].astype(F32)
            return value.astype(BF16)

    row = lax.broadcasted_iota(jnp.int32, (rows, lanes), 0)
    lane = lax.broadcasted_iota(jnp.int32, (rows, lanes), 1)
    starts = [jnp.int32(0)]
    for s in range(segs):
        starts.append(starts[-1] + lens[0, s])

    def mask(s):
        return (row >= starts[s]) & (row < starts[s + 1])

    t_size = half_rows // t_s.shape[2]
    gather_t = Gather(nz, at_z, z, lambda off, h, q: T.at[off, h, pl.ds(q * t_size, t_size)], t_s, t_r)
    gather_c = Gather(nx, at_x, x, lambda off, h, q: C.at[off, h], c_s, c_r)

    def w_piece(off, core, h):
        return Wb.at[pl.ds(1, nx - 1), lax.rem(y + off, ny) * CORES + core, h]

    def g_piece(off, core, h):
        return G.at[CORES * off + core, :, pl.ds(h * (feat // 2), feat // 2)]

    gather_w = Gather(ny, at_y, y, lambda off, h, q: w_piece(off, c, h), wy_s, wy_r, absolute=True)
    gather_g = Gather(ny, at_y, y, lambda off, h, q: g_piece(off, 0, h), gy_s, gy_r)
    scatter_z = Scatter(nz, at_z, z, Pz, zs, zr, rz_s, rz_r)
    scatter_x = Scatter(nx, at_x, x, acc, xs, xr, rx_s, rx_r)

    def w_share(off, h):
        piece = w_piece(off, c, h)
        send(piece, piece, wc_s.at[off, h], wc_r.at[off, h], sibling)

    def g_share(off, h):
        send(g_piece(off, 0, h), g_piece(off, 1, h), gc_s.at[off, h], gc_r.at[off, h], sibling)

    def at_mp(m):
        return (d, lax.rem(x + m // nz, nx) * nz + lax.rem(z + m % nz, nz))

    def from_mp(m):
        return lax.rem(x - m // nz + nx, nx) * nz + lax.rem(z - m % nz + nz, nz)

    fan_a = Fan(
        nx * nz, at_mp,
        lambda m: pairs.at[:, lax.rem(x + m // nz, nx), lax.rem(z + m % nz, nz), d],
        lambda m: S2.at[pl.ds(2 * j, 2)],
        lambda m: S2.at[pl.ds(2 * from_mp(m), 2)], a1_s, a1_r,
    )
    fan_r = Fan(
        nd, lambda m: at_dp(d + m), lambda m: sel.at[m], lambda m: R.at[:, d],
        lambda m: R.at[:, lax.rem(d - m + nd, nd)], a3_s, a3_r,
    )
    fan_lx = Fan(
        nx, lambda k: at_x(x + k), lambda k: Lp.at[lax.rem(x + k, nx)], lambda k: X1.at[k],
        lambda k: X1.at[k], lx_s, lx_r,
    )
    fan_lz = Fan(
        nz, lambda m: at_z(z + m), lambda m: Lz.at[lax.rem(z + m, nz)], lambda m: Z1.at[m],
        lambda m: Z1.at[m], lz_s, lz_r,
    )
    fan_f = Fan(
        nx * nz, at_mp, lambda m: Lf.at[j], lambda m: Lf.at[j], lambda m: Lf.at[from_mp(m)],
        l2_s, l2_r,
    )
    own_w = pltpu.make_async_copy(w.at[x], Wb.at[0], loc.at[0])
    own_a = pltpu.make_async_copy(pairs.at[:, x, z, d], S2.at[pl.ds(2 * j, 2)], loc.at[1])

    def weights():
        for k in range(1, nx):
            send(w.at[lax.rem(x - k + nx, nx), d], Wb.at[k, d], wx_s.at[k], wx_r.at[k], at_x(x - k))
        yield
        for k in range(1, nx):
            arrived(Wb.at[k, d], wx_s.at[k], wx_r.at[k], at_x(x - k))
        steps = gather_w.steps(w_share)
        next(steps)
        for h in range(2):
            w_share(0, h)
        yield
        yield from steps
        own_w.wait()
        for off in range(ny):
            for h in range(2):
                arrived(w_piece(off, 1 - c, h), wc_s.at[off, h], wc_r.at[off, h], sibling)
        yield

    grads = gather_g.steps(g_share)

    def lora():
        fan_a.start()
        yield
        own_a.wait()
        fan_a.wait()
        for m in range(nd):
            other = lax.rem(d + m, nd)
            for s in range(segs):
                sel[m, s] = S2[owner[seg[s, other]]]
        fan_r.start()
        R[:, d] = sel[0]
        yield
        fan_r.wait()
        tok2 = tok[...].reshape(rows, feat)
        cot2 = cot[...].reshape(rows, feat)
        part = jnp.zeros((rows, lanes), F32)
        for s in range(segs):
            pair = R[s].reshape(feat, lanes)
            both = jnp.where(lane < rank, dot(tok2, pair), dot(cot2, pair))
            part = part + jnp.where(mask(s), both, 0.0)
        Lp[...] = part.reshape(Lp.shape)
        fan_lx.start()
        yield
        fan_lx.wait()
        total = Lp[x]
        for k in range(1, nx):
            total = total + X1[k]
        Lz[...] = total.reshape(Lz.shape)
        fan_lz.start()
        yield
        fan_lz.wait()
        total = Lz[z]
        for m in range(1, nz):
            total = total + Z1[m]
        Lf[j] = pltpu.roll(total, rank, 1).astype(BF16)
        fan_f.start()
        yield
        fan_f.wait()
        both = Lf[...].reshape(rows, lanes)
        for s in range(segs):
            Lm[:, s * lanes:(s + 1) * lanes] = jnp.where(mask(s), both, jnp.zeros_like(both))
        g_tok = dot(tok[...].reshape(rows, feat), Lm[...], TN)
        g_cot = dot(cot[...].reshape(rows, feat), Lm[...], TN)
        g_lane = lax.broadcasted_iota(jnp.int32, (feat, lanes), 1)
        for s in range(segs):
            part_s = slice(s * lanes, (s + 1) * lanes)
            G[0, s] = jnp.where(g_lane < rank, g_tok[:, part_s], g_cot[:, part_s]).astype(BF16)
        next(grads)
        for h in range(2):
            g_share(0, h)
        yield

    def fix():
        fix_out = jnp.zeros((rows, feat), F32)
        fix_ig = jnp.zeros((rows, feat), F32)
        for s in range(segs):
            pair = R[s].reshape(feat, lanes)
            mine = Lm[:, s * lanes:(s + 1) * lanes]
            zero = jnp.zeros_like(mine)
            fix_out = fix_out + dot(jnp.where(lane < rank, zero, mine), pair, NT)
            fix_ig = fix_ig + dot(jnp.where(lane < rank, mine, zero), pair, NT)
        acc[0] = acc[0] + fix_out.reshape(2, half_rows, feat)
        Pz[0] = Pz[0] + fix_ig.reshape(2, half_rows, feat)
        yield

    slots = grad.shape[0]
    chunk = min(32, feat)

    def add_grads(i, first):
        off, core = i // CORES, i % CORES
        src = lax.rem(y + off, ny) * CORES + jnp.where(core == 0, c, 1 - c)
        hit = [[(owner[seg[s, src]] == slots * d + q).astype(F32) for s in range(segs)]
               for q in range(slots)]

        def body(r, carry):
            at = pl.ds(pl.multiple_of(r * chunk, chunk), chunk)
            given = [G[i, s, at].astype(F32) for s in range(segs)]
            for q in range(slots):
                value = given[0] * hit[q][0]
                for s in range(1, segs):
                    value = value + given[s] * hit[q][s]
                grad[q, at] = value if first else grad[q, at] + value
            return carry

        lax.fori_loop(0, feat // chunk, body, 0)

    def slots_grad():
        def add(first, count, stride):
            def body(i, carry):
                add_grads(first + i * stride, False)
                return carry

            lax.fori_loop(0, count, body, 0)

        def shared(off):
            for h in range(2):
                arrived(g_piece(off, 1, h), gc_s.at[off, h], gc_r.at[off, h], sibling)

        add_grads(0, True)
        shared(0)
        add(1, 1, 1)
        yield
        if ny > 2:
            add(CORES, 2, CORES * (ny - 2))
            yield
        add(ny, 1, 1)
        for off in range(1, ny):
            shared(off)
        add(CORES + 1, ny - 1, CORES)
        yield

    def partial_ig(off):
        tile = lax.rem(z + off, nz)
        total = jnp.zeros((rows, feat), F32)
        for k in range(nx):
            total = total + dot(C[k].reshape(rows, feat), Wb[k, tile].reshape(feat, feat), NT)
        Pz[off] = total.reshape(2, half_rows, feat)

    def igs():
        def ways(m):
            def body(i, carry):
                partial_ig(m + i * (nz - 2 * m))
                return carry

            lax.fori_loop(0, 2, body, 0)

        partial_ig(nz // 2)
        yield
        for m in range(nz // 2 - 1, 0, -1):
            ways(m)
            yield
        partial_ig(0)
        yield

    def partial_out(m, first):
        tile = lax.rem(z + m, nz)
        block = T[m].reshape(rows, feat)

        def body(k, carry):
            value = dot(block, Wb[k, tile].reshape(feat, feat)).reshape(2, half_rows, feat)
            acc[k] = value if first else acc[k] + value
            return carry

        lax.fori_loop(0, nx, body, 0)

    def outs():
        def ways(m):
            def body(i, carry):
                partial_out(m + i * (nz - 2 * m), False)
                return carry

            lax.fori_loop(0, 2, body, 0)

        partial_out(0, True)
        yield
        for m in range(1, nz // 2):
            ways(m)
            yield
        partial_out(nz // 2, False)
        yield

    own_w.start()
    own_a.start()
    T[0] = tok[...]
    C[0] = cot[...]

    barrier = pltpu.get_barrier_semaphore()
    partners = (
        [at_mp(m) for m in range(1, nx * nz)]
        + [at_dp(d + m) for m in range(1, nd)]
    )
    for device in partners:
        pl.semaphore_signal(barrier, inc=1, device_id=device, device_id_type=pl.DeviceIdType.MESH)
    pl.semaphore_wait(barrier, len(partners))

    tasks = {
        "W": weights(), "T": gather_t.steps(), "C": gather_c.steps(), "L": lora(), "F": fix(), "G": grads,
        "S": slots_grad(), "i": igs(), "I": scatter_z.steps(ig), "o": outs(), "O": scatter_x.steps(out),
    }
    for name in SCHEDULE:
        next(tasks[name], None)
    for task in tasks.values():
        for _ in task:
            pass

    for copy in pending:
        copy.wait_send()


def local(tokens, base_weight, adapter_pairs, owner_map, seg_adapter, seg_lengths, cotangent):
    rows, feat = tokens.shape
    half = rows // 2
    nz = NZ
    nx = lax.axis_size("mp") // nz
    ny = lax.axis_size("dp") // CORES
    nd = ny * CORES
    stored, depth, lanes = adapter_pairs.shape
    segs = seg_lengths.shape[1]
    total_slots = stored * nx * nz
    slots = total_slots // nd
    piece = feat // nd
    lrows = rows // (nx * nz)
    vmem = lambda shape, dtype: pltpu.VMEM(shape, dtype)
    dma = lambda *shape: pltpu.SemaphoreType.DMA(shape)
    ring = lambda n, pieces=1: [dma(2, 2, pieces, n // 2)] * 2
    pair = lambda *shape: [dma(*shape)] * 2
    scratch = [
        vmem((nz, 2, half, feat), BF16),
        vmem((nx, 2, half, feat), BF16),
        vmem((nx, nz, 2, feat // 2, feat), BF16),
        vmem((total_slots, piece, lanes), BF16),
        vmem((nd, segs, piece, lanes), BF16),
        vmem((segs, nd, piece, lanes), BF16),
        vmem((nx, rows // nx, lanes), F32),
        vmem((nx, rows // nx, lanes), F32),
        vmem((nz, lrows, lanes), F32),
        vmem((nz, lrows, lanes), F32),
        vmem((nx * nz, lrows, lanes), BF16),
        vmem((rows, segs * lanes), BF16),
        vmem((nx, 2, half, feat), F32),
        vmem((nz, 2, half, feat), F32),
        vmem((2, 2, nz // 2, half, feat), BF16),
        vmem((2, 2, nz // 2, half, feat), BF16),
        vmem((2, 2, nx // 2, half, feat), BF16),
        vmem((2, 2, nx // 2, half, feat), BF16),
        vmem((nd, segs, feat, lanes), BF16),
        *ring(nz, QT), *ring(nx), *pair(nx), *ring(ny), *pair(ny, 2),
        *pair(nx * nz), *pair(nd), *pair(nx), *pair(nz), *pair(nx * nz),
        *ring(nz, QI), *ring(nx), *ring(ny), *pair(ny, 2), dma(2),
    ]
    in_vmem = pl.BlockSpec(memory_space=pltpu.VMEM)
    in_smem = pl.BlockSpec(memory_space=pltpu.SMEM)
    in_any = pl.BlockSpec(memory_space=pl.ANY)
    out, ig, grad = pl.pallas_call(
        functools.partial(kernel, nx, nz, ny),
        out_shape=[
            pltpu.VMEM((2, half, feat), BF16),
            pltpu.VMEM((2, half, feat), BF16),
            pltpu.VMEM((slots, feat, lanes), F32),
        ],
        in_specs=[in_vmem, in_vmem, in_any, in_any, in_smem, in_smem, in_smem],
        out_specs=[in_vmem] * 3,
        scratch_shapes=scratch,
        compiler_params=pltpu.CompilerParams(
            collective_id=0, has_side_effects=True, vmem_limit_bytes=56 * 1024 * 1024
        ),
    )(
        tokens.reshape(2, half, feat),
        cotangent.reshape(2, half, feat),
        base_weight.reshape(nx, nz, 2, feat // 2, feat),
        adapter_pairs.reshape(stored, nx, nz, nd, piece, lanes),
        owner_map,
        seg_adapter.T,
        seg_lengths,
    )
    return out.reshape(rows, feat), ig.reshape(rows, feat), grad


def solution(mesh):
    in_specs = (
        P("dp", "mp"),
        P(None, "mp"),
        P("mp", None, None),
        P(),
        P(),
        P("dp", None),
        P("dp", "mp"),
    )
    out_specs = (P("dp", "mp"), P("dp", "mp"), P("dp", "mp", None))
    return jax.shard_map(local, mesh=mesh, in_specs=in_specs, out_specs=out_specs, check_vma=False)
```

time: 613 us -> 81.4 us (0.13)
  waiting for transfers between devices: 408 us -> 0 us
  blocking collectives: 125 us -> 0 us
  Pallas kernels: 0 us -> 78.3 us
  matrix products: 26.3 us -> 0 us
  local copies, waits for them, and re-layouts: 21.6 us -> 2.38 us
  between operations: 15.6 us -> 0.64 us
  starting transfers between devices: 12.3 us -> 0 us
    reduce_scatter x2 -> x0, waiting for transfers between devices: 301 us -> none  [the longest x1 243 us: local(): lax.psum_scatter(lax.dot_general(weight_rows, cotangent, (((1,), (1,)), (...]
    psum x1 -> x0, blocking collectives: 125 us -> none  [local(): low_sum = lax.psum(low_part, 'mp')]
    all_to_all x1 -> x0, waiting for transfers between devices: 106 us -> none  [local(): lax.all_to_all(adapter_pairs, 'mp', split_axis=1, concat_axis=0, tiled=True)]
    pallas_call x0 -> x1, Pallas kernels: none -> 78.3 us  [local(): pl.pallas_call(functools.partial(kernel, nx, nz, ny), out_shape=[pltpu.VM...]
    dot_general x9 -> x0, matrix products: 26.3 us -> none  [the longest x1 10.3 us: local(): lax.dot_general(weight_rows, cotangent, (((1,), (1,)), ((), ())), preferr...]
    all_to_all x1 -> x0, starting transfers between devices: 12.1 us -> none  [local(): lax.all_to_all(adapter_pairs, 'mp', split_axis=1, concat_axis=0, tiled=True)]
    unnamed x13 -> x3, local copies, waits for them, and re-layouts: 13.4 us -> 2.38 us
  transfers between devices with their start and end apart: 4 -> 0, of which waited for: 3 -> 0; matrix products, arithmetic and copies ran while one was open for 8% -> 0% of each run, Pallas kernels for 0% -> 0%
where the time goes in v2:
time: 81.4 us; the launch traced here: 81.3 us
  Pallas kernels  78.3 us (96%)
  local copies, waits for them, and re-layouts  2.38 us (3%)
    pallas_call x1, Pallas kernels, local(): pl.pallas_call(functools.partial(kernel, nx, nz, ny), out_shape=[pltpu.VM...  78.3 us
    unnamed x3, local copies, waits for them, and re-layouts  2.38 us

profile of v2, /device:TPU:1, one launch (start us, length us, event | category | flops | bytes accessed | tf_op | source)
XLA Modules:
  0.0 81.3 jit_solution(4227013771715902135)
XLA Ops:
  0.6 78.3 %shard_map.94 = (bf16[2,256,256]{2,1,0:T(8,128)(2,1)S(1)}, bf16[2,256,256]{2,1,0:T(8,128)(2,1)S(1)}, f32[8,256,128]{2,1,0:T(8,128)S(1)}) custom-call(bf16[2,256,256]{2,1,0:T(8,128)(2,1)} %bitcast.11, bf16[2,256,256]{2,1,0:T(8,128)(2,1)} %bitcast.12, bf16[4,8,2,128,256]{4,3,2,1,0:T(8,128)(2,1)} %bitcast.9, bf16[2,4,8,8,32,128]{5,4,3,2,1,0:T(8,128)(2,1)} %bitcast.10, ...), custom_call_target="tpu_custom_call" | custom-call | tf_op jit(solution)/shard_map/pallas_call | solution.py:504
  78.9 0.7 copy.13
  79.6 0.7 copy.14
  80.3 1.0 %copy.15 = f32[8,256,128]{2,1,0:T(8,128)} copy(f32[8,256,128]{2,1,0:T(8,128)S(1)} %get-tuple-element.11) | data formatting | bytes 2097152

commit v3 on v2

--- a/solution.py
+++ b/solution.py
@@ -13,7 +13,7 @@
 QI = 1
 F32 = jnp.float32
 BF16 = jnp.bfloat16
-SCHEDULE = "WLTWCLWCTWTLCTTWWLCiiTooITLIoIoiTLoIOIOGiOISiGIFGSSOI"
+SCHEDULE = "LTWCLCWTCLTTWLTLCWTWLWiIiIooToILiITooOIOiiSGIOGISGFSOI"
 NT = (((1,), (1,)), ((), ()))
 TN = (((0,), (0,)), ((), ()))
 
@@ -32,7 +32,7 @@
     out, ig, grad,
     T, C, Wb, S2, sel, R, Lp, X1, Lz, Z1, Lf, Lm, acc, Pz, zs, zr, xs, xr, G,
     t_s, t_r, c_s, c_r, wx_s, wx_r, wy_s, wy_r, wc_s, wc_r,
-    a1_s, a1_r, a3_s, a3_r, lx_s, lx_r, lz_s, lz_r, l2_s, l2_r,
+    a1_s, a1_r, a3_s, a3_r, lx_s, lx_r, lz_s, lz_r, fz_s, fz_r, fx_s, fx_r,
     rz_s, rz_r, rx_s, rx_r, gy_s, gy_r, gc_s, gc_r, loc,
 ):
     nd = ny * CORES
@@ -241,10 +241,16 @@
         nz, lambda m: at_z(z + m), lambda m: Lz.at[lax.rem(z + m, nz)], lambda m: Z1.at[m],
         lambda m: Z1.at[m], lz_s, lz_r,
     )
-    fan_f = Fan(
-        nx * nz, at_mp, lambda m: Lf.at[j], lambda m: Lf.at[j], lambda m: Lf.at[from_mp(m)],
-        l2_s, l2_r,
-    )
+    fan_fz = Fan(
+        nz, lambda m: at_z(z + m), lambda m: Lf.at[x, z], lambda m: Lf.at[x, z],
+        lambda m: Lf.at[x, lax.rem(z - m + nz, nz)], fz_s, fz_r,
+    )
+    fan_fx = Fan(
+        nx, lambda k: at_x(x + k), lambda k: Lf.at[x], lambda k: Lf.at[x],
+        lambda k: Lf.at[lax.rem(x - k + nx, nx)], fx_s, fx_r,
+    )
+    own_t = pltpu.make_async_copy(tok, T.at[0], loc.at[2])
+    own_c = pltpu.make_async_copy(cot, C.at[0], loc.at[3])
     own_w = pltpu.make_async_copy(w.at[x], Wb.at[0], loc.at[0])
     own_a = pltpu.make_async_copy(pairs.at[:, x, z, d], S2.at[pl.ds(2 * j, 2)], loc.at[1])
 
@@ -281,8 +287,8 @@
         R[:, d] = sel[0]
         yield
         fan_r.wait()
-        tok2 = tok[...].reshape(rows, feat)
-        cot2 = cot[...].reshape(rows, feat)
+        tok2 = T[0].reshape(rows, feat)
+        cot2 = C[0].reshape(rows, feat)
         part = jnp.zeros((rows, lanes), F32)
         for s in range(segs):
             pair = R[s].reshape(feat, lanes)
@@ -302,15 +308,18 @@
         total = Lz[z]
         for m in range(1, nz):
             total = total + Z1[m]
-        Lf[j] = pltpu.roll(total, rank, 1).astype(BF16)
-        fan_f.start()
-        yield
-        fan_f.wait()
+        Lf[x, z] = pltpu.roll(total, rank, 1).astype(BF16)
+        fan_fz.start()
+        yield
+        fan_fz.wait()
+        fan_fx.start()
+        yield
+        fan_fx.wait()
         both = Lf[...].reshape(rows, lanes)
         for s in range(segs):
             Lm[:, s * lanes:(s + 1) * lanes] = jnp.where(mask(s), both, jnp.zeros_like(both))
-        g_tok = dot(tok[...].reshape(rows, feat), Lm[...], TN)
-        g_cot = dot(cot[...].reshape(rows, feat), Lm[...], TN)
+        g_tok = dot(T[0].reshape(rows, feat), Lm[...], TN)
+        g_cot = dot(C[0].reshape(rows, feat), Lm[...], TN)
         g_lane = lax.broadcasted_iota(jnp.int32, (feat, lanes), 1)
         for s in range(segs):
             part_s = slice(s * lanes, (s + 1) * lanes)
@@ -375,8 +384,11 @@
             yield
         add(ny, 1, 1)
         for off in range(1, ny):
-            shared(off)
-        add(CORES + 1, ny - 1, CORES)
+            if 2 * off != ny:
+                shared(off)
+        add(CORES + 1, 2 if ny > 2 else 0, CORES * (ny - 2))
+        shared(ny // 2)
+        add(ny + 1, 1, 1)
         yield
 
     def partial_ig(off):
@@ -429,10 +441,10 @@
         partial_out(nz // 2, False)
         yield
 
+    own_t.start()
+    own_c.start()
+    own_a.start()
     own_w.start()
-    own_a.start()
-    T[0] = tok[...]
-    C[0] = cot[...]
 
     barrier = pltpu.get_barrier_semaphore()
     partners = (
@@ -442,6 +454,8 @@
     for device in partners:
         pl.semaphore_signal(barrier, inc=1, device_id=device, device_id_type=pl.DeviceIdType.MESH)
     pl.semaphore_wait(barrier, len(partners))
+    own_t.wait()
+    own_c.wait()
 
     tasks = {
         "W": weights(), "T": gather_t.steps(), "C": gather_c.steps(), "L": lora(), "F": fix(), "G": grads,
@@ -485,7 +499,7 @@
         vmem((nx, rows // nx, lanes), F32),
         vmem((nz, lrows, lanes), F32),
         vmem((nz, lrows, lanes), F32),
-        vmem((nx * nz, lrows, lanes), BF16),
+        vmem((nx, nz, lrows, lanes), BF16),
         vmem((rows, segs * lanes), BF16),
         vmem((nx, 2, half, feat), F32),
         vmem((nz, 2, half, feat), F32),
@@ -495,8 +509,8 @@
         vmem((2, 2, nx // 2, half, feat), BF16),
         vmem((nd, segs, feat, lanes), BF16),
         *ring(nz, QT), *ring(nx), *pair(nx), *ring(ny), *pair(ny, 2),
-        *pair(nx * nz), *pair(nd), *pair(nx), *pair(nz), *pair(nx * nz),
-        *ring(nz, QI), *ring(nx), *ring(ny), *pair(ny, 2), dma(2),
+        *pair(nx * nz), *pair(nd), *pair(nx), *pair(nz), *pair(nz), *pair(nx),
+        *ring(nz, QI), *ring(nx), *ring(ny), *pair(ny, 2), dma(4),
     ]
     in_vmem = pl.BlockSpec(memory_space=pltpu.VMEM)
     in_smem = pl.BlockSpec(memory_space=pltpu.SMEM)
@@ -508,7 +522,7 @@
             pltpu.VMEM((2, half, feat), BF16),
             pltpu.VMEM((slots, feat, lanes), F32),
         ],
-        in_specs=[in_vmem, in_vmem, in_any, in_any, in_smem, in_smem, in_smem],
+        in_specs=[in_any] * 4 + [in_smem, in_smem, in_smem],
         out_specs=[in_vmem] * 3,
         scratch_shapes=scratch,
         compiler_params=pltpu.CompilerParams(

time: 81.4 us -> 77.5 us (0.952)
  Pallas kernels: 78.3 us -> 74.1 us
    pallas_call x1, Pallas kernels: 78.3 us -> 74.1 us  [local(): pl.pallas_call(functools.partial(kernel, nx, nz, ny), out_shape=[pltpu.VM...]
where the time goes in v3:
time: 77.5 us; the launch traced here: 77.2 us
  Pallas kernels  74.1 us (96%)
  local copies, waits for them, and re-layouts  2.38 us (3%)
    pallas_call x1, Pallas kernels, local(): pl.pallas_call(functools.partial(kernel, nx, nz, ny), out_shape=[pltpu.VM...  74.1 us
    unnamed x3, local copies, waits for them, and re-layouts  2.38 us

profile of v3, /device:TPU:1, one launch (start us, length us, event | category | flops | bytes accessed | tf_op | source)
XLA Modules:
  0.0 77.2 jit_solution(18021098738350402586)
XLA Ops:
  0.6 74.1 %shard_map.94 = (bf16[2,256,256]{2,1,0:T(8,128)(2,1)S(1)}, bf16[2,256,256]{2,1,0:T(8,128)(2,1)S(1)}, f32[8,256,128]{2,1,0:T(8,128)S(1)}) custom-call(bf16[2,256,256]{2,1,0:T(8,128)(2,1)} %bitcast.11, bf16[2,256,256]{2,1,0:T(8,128)(2,1)} %bitcast.12, bf16[4,8,2,128,256]{4,3,2,1,0:T(8,128)(2,1)} %bitcast.9, bf16[2,4,8,8,32,128]{5,4,3,2,1,0:T(8,128)(2,1)} %bitcast.10, ...), custom_call_target="tpu_custom_call" | custom-call | tf_op jit(solution)/shard_map/pallas_call | solution.py:518
  74.8 0.7 copy.13
  75.5 0.7 copy.14
  76.2 1.0 %copy.15 = f32[8,256,128]{2,1,0:T(8,128)} copy(f32[8,256,128]{2,1,0:T(8,128)S(1)} %get-tuple-element.11) | data formatting | bytes 2097152

commit v4 on v3

--- a/solution.py
+++ b/solution.py
@@ -13,7 +13,7 @@
 QI = 1
 F32 = jnp.float32
 BF16 = jnp.bfloat16
-SCHEDULE = "LTWCLCWTCLTTWLTLCWTWLWiIiIooToILiITooOIOiiSGIOGISGFSOI"
+SCHEDULE = "WLTCWCTLTWWTLTWTWCoCiLiIoLTIoLTIioILIoOiOSGIiIOGFSGSOI"
 NT = (((1,), (1,)), ((), ()))
 TN = (((0,), (0,)), ((), ()))
 
@@ -28,13 +28,15 @@
 
 def kernel(
     nx, nz, ny,
-    tok, cot, w, pairs, owner, seg, lens,
-    out, ig, grad,
-    T, C, Wb, S2, sel, R, Lp, X1, Lz, Z1, Lf, Lm, acc, Pz, zs, zr, xs, xr, G,
+    tok, cot, w, pairs, owner_in, seg_in, lens_in,
+    both, grad,
+    owner, seg, lens, T, C, Wb, S2, sel, R, Lp, X1, Lz, Z1, Lf, Lm, acc, Pz, zs, zr, xs, xr, G,
     t_s, t_r, c_s, c_r, wx_s, wx_r, wy_s, wy_r, wc_s, wc_r,
     a1_s, a1_r, a3_s, a3_r, lx_s, lx_r, lz_s, lz_r, fz_s, fz_r, fx_s, fx_r,
     rz_s, rz_r, rx_s, rx_r, gy_s, gy_r, gc_s, gc_r, loc,
 ):
+    out = both.at[pl.ds(0, 2)]
+    ig = both.at[pl.ds(2, 2)]
     nd = ny * CORES
     d = lax.axis_index("dp")
     j = lax.axis_index("mp")
@@ -189,8 +191,6 @@
     row = lax.broadcasted_iota(jnp.int32, (rows, lanes), 0)
     lane = lax.broadcasted_iota(jnp.int32, (rows, lanes), 1)
     starts = [jnp.int32(0)]
-    for s in range(segs):
-        starts.append(starts[-1] + lens[0, s])
 
     def mask(s):
         return (row >= starts[s]) & (row < starts[s + 1])
@@ -249,6 +249,10 @@
         nx, lambda k: at_x(x + k), lambda k: Lf.at[x], lambda k: Lf.at[x],
         lambda k: Lf.at[lax.rem(x - k + nx, nx)], fx_s, fx_r,
     )
+    own_s = [
+        pltpu.make_async_copy(src, dst, loc.at[4 + i])
+        for i, (src, dst) in enumerate(((owner_in, owner), (seg_in, seg), (lens_in, lens)))
+    ]
     own_t = pltpu.make_async_copy(tok, T.at[0], loc.at[2])
     own_c = pltpu.make_async_copy(cot, C.at[0], loc.at[3])
     own_w = pltpu.make_async_copy(w.at[x], Wb.at[0], loc.at[0])
@@ -301,13 +305,13 @@
         total = Lp[x]
         for k in range(1, nx):
             total = total + X1[k]
-        Lz[...] = total.reshape(Lz.shape)
+        Lz[...] = total.reshape(Lz.shape).astype(BF16)
         fan_lz.start()
         yield
         fan_lz.wait()
-        total = Lz[z]
+        total = Lz[z].astype(F32)
         for m in range(1, nz):
-            total = total + Z1[m]
+            total = total + Z1[m].astype(F32)
         Lf[x, z] = pltpu.roll(total, rank, 1).astype(BF16)
         fan_fz.start()
         yield
@@ -441,6 +445,8 @@
         partial_out(nz // 2, False)
         yield
 
+    for copy in own_s:
+        copy.start()
     own_t.start()
     own_c.start()
     own_a.start()
@@ -454,8 +460,12 @@
     for device in partners:
         pl.semaphore_signal(barrier, inc=1, device_id=device, device_id_type=pl.DeviceIdType.MESH)
     pl.semaphore_wait(barrier, len(partners))
+    for copy in own_s:
+        copy.wait()
     own_t.wait()
     own_c.wait()
+    for s in range(segs):
+        starts.append(starts[-1] + lens[0, s])
 
     tasks = {
         "W": weights(), "T": gather_t.steps(), "C": gather_c.steps(), "L": lora(), "F": fix(), "G": grads,
@@ -489,6 +499,9 @@
     ring = lambda n, pieces=1: [dma(2, 2, pieces, n // 2)] * 2
     pair = lambda *shape: [dma(*shape)] * 2
     scratch = [
+        pltpu.SMEM(owner_map.shape, jnp.int32),
+        pltpu.SMEM((segs, nd), jnp.int32),
+        pltpu.SMEM(seg_lengths.shape, jnp.int32),
         vmem((nz, 2, half, feat), BF16),
         vmem((nx, 2, half, feat), BF16),
         vmem((nx, nz, 2, feat // 2, feat), BF16),
@@ -497,8 +510,8 @@
         vmem((segs, nd, piece, lanes), BF16),
         vmem((nx, rows // nx, lanes), F32),
         vmem((nx, rows // nx, lanes), F32),
-        vmem((nz, lrows, lanes), F32),
-        vmem((nz, lrows, lanes), F32),
+        vmem((nz, lrows, lanes), BF16),
+        vmem((nz, lrows, lanes), BF16),
         vmem((nx, nz, lrows, lanes), BF16),
         vmem((rows, segs * lanes), BF16),
         vmem((nx, 2, half, feat), F32),
@@ -510,20 +523,18 @@
         vmem((nd, segs, feat, lanes), BF16),
         *ring(nz, QT), *ring(nx), *pair(nx), *ring(ny), *pair(ny, 2),
         *pair(nx * nz), *pair(nd), *pair(nx), *pair(nz), *pair(nz), *pair(nx),
-        *ring(nz, QI), *ring(nx), *ring(ny), *pair(ny, 2), dma(4),
+        *ring(nz, QI), *ring(nx), *ring(ny), *pair(ny, 2), dma(7),
     ]
     in_vmem = pl.BlockSpec(memory_space=pltpu.VMEM)
-    in_smem = pl.BlockSpec(memory_space=pltpu.SMEM)
     in_any = pl.BlockSpec(memory_space=pl.ANY)
-    out, ig, grad = pl.pallas_call(
+    both, grad = pl.pallas_call(
         functools.partial(kernel, nx, nz, ny),
         out_shape=[
-            pltpu.VMEM((2, half, feat), BF16),
-            pltpu.VMEM((2, half, feat), BF16),
+            pltpu.VMEM((4, half, feat), BF16),
             pltpu.VMEM((slots, feat, lanes), F32),
         ],
-        in_specs=[in_any] * 4 + [in_smem, in_smem, in_smem],
-        out_specs=[in_vmem] * 3,
+        in_specs=[in_any] * 7,
+        out_specs=[in_vmem] * 2,
         scratch_shapes=scratch,
         compiler_params=pltpu.CompilerParams(
             collective_id=0, has_side_effects=True, vmem_limit_bytes=56 * 1024 * 1024
@@ -537,7 +548,8 @@
         seg_adapter.T,
         seg_lengths,
     )
-    return out.reshape(rows, feat), ig.reshape(rows, feat), grad
+    both = both.reshape(2, rows, feat)
+    return both[0], both[1], grad
 
 
 def solution(mesh):

time: 77.5 us -> 75.5 us (0.974)
  Pallas kernels: 74.1 us -> 73 us
    unnamed x3 -> x1, local copies, waits for them, and re-layouts: 2.38 us -> 0.97 us
    pallas_call x1, Pallas kernels: 74.1 us -> 73 us  [local(): pl.pallas_call(functools.partial(kernel, nx, nz, ny), out_shape=[pltpu.VM...]
    slice x0 -> x1, local copies, waits for them, and re-layouts: none -> 0.82 us  [local(): return (both[0], both[1], grad)]
where the time goes in v4:
time: 75.5 us
  Pallas kernels  73 us (97%)
  local copies, waits for them, and re-layouts  1.79 us (2%)
    pallas_call x1, Pallas kernels, local(): pl.pallas_call(functools.partial(kernel, nx, nz, ny), out_shape=[pltpu.VM...  73 us

profile of v4, /device:TPU:1, one launch (start us, length us, event | category | flops | bytes accessed | tf_op | source)
XLA Modules:
  0.0 75.5 jit_solution(16238538210075290498)
XLA Ops:
  0.6 73.0 %shard_map.94 = (bf16[4,256,256]{2,1,0:T(8,128)(2,1)S(1)}, f32[8,256,128]{2,1,0:T(8,128)S(1)}) custom-call(bf16[2,256,256]{2,1,0:T(8,128)(2,1)} %bitcast.11, bf16[2,256,256]{2,1,0:T(8,128)(2,1)} %bitcast.12, bf16[4,8,2,128,256]{4,3,2,1,0:T(8,128)(2,1)} %bitcast.7, bf16[2,4,8,8,32,128]{5,4,3,2,1,0:T(8,128)(2,1)} %bitcast.8, s32[64]{0:T(128)} %owner_in.1, ...), custom_call_target="tpu_custom_call" | custom-call | tf_op jit(solution)/shard_map/pallas_call | solution.py:530
  73.7 0.8 %fusion = (bf16[2,256,256]{2,1,0:T(8,128)(2,1)}, bf16[2,256,256]{2,1,0:T(8,128)(2,1)}) fusion(bf16[4,256,256]{2,1,0:T(8,128)(2,1)S(1)} %get-tuple-element.5), kind=kLoop, calls=%fused_computation | loop fusion | bytes 1048576 | tf_op jit(solution)/shard_map/slice | solution.py:552
  74.5 1.0 %copy.11 = f32[8,256,128]{2,1,0:T(8,128)} copy(f32[8,256,128]{2,1,0:T(8,128)S(1)} %get-tuple-element.11) | data formatting | bytes 2097152

commit v5 on v4

--- a/solution.py
+++ b/solution.py
@@ -83,7 +83,10 @@
             self.ssem, self.rsem = ssem, rsem
 
         def start(self):
-            for m in range(1, self.count):
+            def rank_of(m):
+                return -min(m % nz, nz - m % nz), m // nz
+
+            for m in sorted(range(1, self.count), key=rank_of):
                 send(self.src(m), self.dst(m), self.ssem.at[m], self.rsem.at[m], self.at(m))
 
         def wait(self):

time: 75.5 us -> 73.4 us (0.972)
  Pallas kernels: 73 us -> 70.9 us
    pallas_call x1, Pallas kernels: 73 us -> 70.9 us  [local(): pl.pallas_call(functools.partial(kernel, nx, nz, ny), out_shape=[pltpu.VM...]
where the time goes in v5:
time: 73.4 us; the launch traced here: 73.3 us
  Pallas kernels  70.9 us (97%)
  local copies, waits for them, and re-layouts  1.79 us (2%)
    pallas_call x1, Pallas kernels, local(): pl.pallas_call(functools.partial(kernel, nx, nz, ny), out_shape=[pltpu.VM...  70.9 us

profile of v5, /device:TPU:1, one launch (start us, length us, event | category | flops | bytes accessed | tf_op | source)
XLA Modules:
  0.0 73.3 jit_solution(15335089226043930497)
XLA Ops:
  0.6 70.9 %shard_map.94 = (bf16[4,256,256]{2,1,0:T(8,128)(2,1)S(1)}, f32[8,256,128]{2,1,0:T(8,128)S(1)}) custom-call(bf16[2,256,256]{2,1,0:T(8,128)(2,1)} %bitcast.11, bf16[2,256,256]{2,1,0:T(8,128)(2,1)} %bitcast.12, bf16[4,8,2,128,256]{4,3,2,1,0:T(8,128)(2,1)} %bitcast.7, bf16[2,4,8,8,32,128]{5,4,3,2,1,0:T(8,128)(2,1)} %bitcast.8, s32[64]{0:T(128)} %owner_in.1, ...), custom_call_target="tpu_custom_call" | custom-call | tf_op jit(solution)/shard_map/pallas_call | solution.py:533
  71.5 0.8 %fusion = (bf16[2,256,256]{2,1,0:T(8,128)(2,1)}, bf16[2,256,256]{2,1,0:T(8,128)(2,1)}) fusion(bf16[4,256,256]{2,1,0:T(8,128)(2,1)S(1)} %get-tuple-element.5), kind=kLoop, calls=%fused_computation | loop fusion | bytes 1048576 | tf_op jit(solution)/shard_map/slice | solution.py:555
  72.3 1.0 %copy.11 = f32[8,256,128]{2,1,0:T(8,128)} copy(f32[8,256,128]{2,1,0:T(8,128)S(1)} %get-tuple-element.11) | data formatting | bytes 2097152

commit v6 on v5

--- a/solution.py
+++ b/solution.py
@@ -13,7 +13,7 @@
 QI = 1
 F32 = jnp.float32
 BF16 = jnp.bfloat16
-SCHEDULE = "WLTCWCTLTWWTLTWTWCoCiLiIoLTIoLTIioILIoOiOSGIiIOGFSGSOI"
+SCHEDULE = "WLTWCTLWTCTLWTWCTWCioLIioTLIioTLIooOILIOSiOiIGFIGSOGSI"
 NT = (((1,), (1,)), ((), ()))
 TN = (((0,), (0,)), ((), ()))
 

time: 73.4 us -> 73.1 us (level)
  no operation moved by 1% of the time
where the time goes in v6:
time: 73.1 us
  Pallas kernels  70.6 us (97%)
  local copies, waits for them, and re-layouts  1.79 us (2%)
    pallas_call x1, Pallas kernels, local(): pl.pallas_call(functools.partial(kernel, nx, nz, ny), out_shape=[pltpu.VM...  70.6 us

profile of v6, /device:TPU:1, one launch (start us, length us, event | category | flops | bytes accessed | tf_op | source)
XLA Modules:
  0.0 73.1 jit_solution(15706698529134951176)
XLA Ops:
  0.6 70.6 %shard_map.94 = (bf16[4,256,256]{2,1,0:T(8,128)(2,1)S(1)}, f32[8,256,128]{2,1,0:T(8,128)S(1)}) custom-call(bf16[2,256,256]{2,1,0:T(8,128)(2,1)} %bitcast.11, bf16[2,256,256]{2,1,0:T(8,128)(2,1)} %bitcast.12, bf16[4,8,2,128,256]{4,3,2,1,0:T(8,128)(2,1)} %bitcast.7, bf16[2,4,8,8,32,128]{5,4,3,2,1,0:T(8,128)(2,1)} %bitcast.8, s32[64]{0:T(128)} %owner_in.1, ...), custom_call_target="tpu_custom_call" | custom-call | tf_op jit(solution)/shard_map/pallas_call | solution.py:533
  71.3 0.8 %fusion = (bf16[2,256,256]{2,1,0:T(8,128)(2,1)}, bf16[2,256,256]{2,1,0:T(8,128)(2,1)}) fusion(bf16[4,256,256]{2,1,0:T(8,128)(2,1)S(1)} %get-tuple-element.5), kind=kLoop, calls=%fused_computation | loop fusion | bytes 1048576 | tf_op jit(solution)/shard_map/slice | solution.py:555
  72.1 1.0 %copy.11 = f32[8,256,128]{2,1,0:T(8,128)} copy(f32[8,256,128]{2,1,0:T(8,128)S(1)} %get-tuple-element.11) | data formatting | bytes 2097152

commit v7 on v6

--- a/solution.py
+++ b/solution.py
@@ -87,7 +87,10 @@
                 return -min(m % nz, nz - m % nz), m // nz
 
             for m in sorted(range(1, self.count), key=rank_of):
-                send(self.src(m), self.dst(m), self.ssem.at[m], self.rsem.at[m], self.at(m))
+                self.send(m)
+
+        def send(self, m):
+            send(self.src(m), self.dst(m), self.ssem.at[m], self.rsem.at[m], self.at(m))
 
         def wait(self):
             for m in range(1, self.count):
@@ -262,7 +265,7 @@
     own_a = pltpu.make_async_copy(pairs.at[:, x, z, d], S2.at[pl.ds(2 * j, 2)], loc.at[1])
 
     def weights():
-        for k in range(1, nx):
+        for k in sorted(range(1, nx), key=lambda k: -min(k, nx - k)):
             send(w.at[lax.rem(x - k + nx, nx), d], Wb.at[k, d], wx_s.at[k], wx_r.at[k], at_x(x - k))
         yield
         for k in range(1, nx):
@@ -286,12 +289,13 @@
         yield
         own_a.wait()
         fan_a.wait()
-        for m in range(nd):
+        for m in range(1, nd):
             other = lax.rem(d + m, nd)
             for s in range(segs):
                 sel[m, s] = S2[owner[seg[s, other]]]
-        fan_r.start()
-        R[:, d] = sel[0]
+            fan_r.send(m)
+        for s in range(segs):
+            R[s, d] = S2[owner[seg[s, d]]]
         yield
         fan_r.wait()
         tok2 = T[0].reshape(rows, feat)

time: 73.1 us -> 73.2 us (level)
  no operation moved by 1% of the time
where the time goes in v7:
time: 73.2 us; the launch traced here: 73.1 us
  Pallas kernels  70.7 us (97%)
  local copies, waits for them, and re-layouts  1.79 us (2%)
    pallas_call x1, Pallas kernels, local(): pl.pallas_call(functools.partial(kernel, nx, nz, ny), out_shape=[pltpu.VM...  70.7 us

profile of v7, /device:TPU:1, one launch (start us, length us, event | category | flops | bytes accessed | tf_op | source)
XLA Modules:
  0.0 73.1 jit_solution(2243382092704078928)
XLA Ops:
  0.6 70.7 %shard_map.94 = (bf16[4,256,256]{2,1,0:T(8,128)(2,1)S(1)}, f32[8,256,128]{2,1,0:T(8,128)S(1)}) custom-call(bf16[2,256,256]{2,1,0:T(8,128)(2,1)} %bitcast.11, bf16[2,256,256]{2,1,0:T(8,128)(2,1)} %bitcast.12, bf16[4,8,2,128,256]{4,3,2,1,0:T(8,128)(2,1)} %bitcast.7, bf16[2,4,8,8,32,128]{5,4,3,2,1,0:T(8,128)(2,1)} %bitcast.8, s32[64]{0:T(128)} %owner_in.1, ...), custom_call_target="tpu_custom_call" | custom-call | tf_op jit(solution)/shard_map/pallas_call | solution.py:537
  71.4 0.8 %fusion = (bf16[2,256,256]{2,1,0:T(8,128)(2,1)}, bf16[2,256,256]{2,1,0:T(8,128)(2,1)}) fusion(bf16[4,256,256]{2,1,0:T(8,128)(2,1)S(1)} %get-tuple-element.5), kind=kLoop, calls=%fused_computation | loop fusion | bytes 1048576 | tf_op jit(solution)/shard_map/slice | solution.py:559
  72.2 1.0 %copy.11 = f32[8,256,128]{2,1,0:T(8,128)} copy(f32[8,256,128]{2,1,0:T(8,128)S(1)} %get-tuple-element.11) | data formatting | bytes 2097152
